TPU v7x, 32 devices: a whole 2x2x4 slice. The times are simulated.
32 devices in a mesh: fsdp: 8 (over y, x, core), seq: 4 (over z).
Axes of the slice: x: 2, y: 2, z: 4, core: 2. Of those that a mesh axis runs over, the one named last changes fastest.
Arguments:
- block_in: bfloat16 [20480, 640], P(('fsdp', 'seq')), may hold values from -134 to 134
- query_weight: bfloat16 [640, 1024], P('fsdp'), may hold values from -0.25 to 0.25
- key_weight: bfloat16 [640, 256], P('fsdp'), may hold values from -0.25 to 0.25
- value_weight: bfloat16 [640, 256], P('fsdp'), may hold values from -0.25 to 0.25
- output_weight: bfloat16 [1024, 640], P('fsdp'), may hold values from -0.1875 to 0.1875
- gate_weight: bfloat16 [640, 2048], P('fsdp'), may hold values from -0.25 to 0.25
- up_weight: bfloat16 [640, 2048], P('fsdp'), may hold values from -0.25 to 0.25
- down_weight: bfloat16 [2048, 640], P('fsdp'), may hold values from -0.125 to 0.125
- attention_norm: bfloat16 [640], P('fsdp'), may hold values from 0.099609375 to 1.8984375
- query_norm: bfloat16 [256], P('fsdp'), may hold values from 0.099609375 to 1.8984375
- key_norm: bfloat16 [256], P('fsdp'), may hold values from 0.099609375 to 1.8984375
- post_attention_norm: bfloat16 [640], P('fsdp'), may hold values from 0.099609375 to 1.8984375
- feedforward_norm: bfloat16 [640], P('fsdp'), may hold values from 0.099609375 to 1.8984375
- post_feedforward_norm: bfloat16 [640], P('fsdp'), may hold values from 0.099609375 to 1.8984375
- grad_out: bfloat16 [20480, 640], P(('fsdp', 'seq')), may hold values from -6 to 6
Outputs:
- block_out: bfloat16 [20480, 640], P(('fsdp', 'seq'))
- grad_in: bfloat16 [20480, 640], P(('fsdp', 'seq'))
- grad_query_weight: float32 [640, 1024], P('fsdp')
- grad_key_weight: float32 [640, 256], P('fsdp')
- grad_value_weight: float32 [640, 256], P('fsdp')
- grad_output_weight: float32 [1024, 640], P('fsdp')
- grad_gate_weight: float32 [640, 2048], P('fsdp')
- grad_up_weight: float32 [640, 2048], P('fsdp')
- grad_down_weight: float32 [2048, 640], P('fsdp')
- grad_attention_norm: float32 [640], P('fsdp')
- grad_query_norm: float32 [256], P('fsdp')
- grad_key_norm: float32 [256], P('fsdp')
- grad_post_attention_norm: float32 [640], P('fsdp')
- grad_feedforward_norm: float32 [640], P('fsdp')
- grad_post_feedforward_norm: float32 [640], P('fsdp')
All inputs are finite; a program needn't handle non-finite values.
Results may differ from a plain program's by a relative error of at most 0.018.
Values may be sent and summed in bfloat16 or wider, within the bound.
A program may use at most 128 MiB of HBM per device.

v0:
```python
import jax
import jax.numpy as jnp
from jax import lax
from jax.sharding import PartitionSpec as P

epsilon = 1e-06
rope_base = 1000000.0
negative = -1e30


def rms_scale(values, gain_row):
    return values * lax.rsqrt(jnp.mean(values * values, -1, keepdims=True) + epsilon) * gain_row


def rotate(values, cosine_table, sine_table):
    half_width = values.shape[-1] // 2
    first_half = values[..., :half_width]
    second = values[..., half_width:]
    return jnp.concatenate(
        [
            first_half * cosine_table - second * sine_table,
            second * cosine_table + first_half * sine_table,
        ],
        -1,
    )


def angles_for(positions, width):
    half_width = width // 2
    frequency = rope_base ** (-(jnp.arange(half_width).astype(jnp.float32) * 2.0 / width))
    angles = positions[:, None] * frequency[None, :]
    return (jnp.cos(angles), jnp.sin(angles))


def gelu_product(gate_lin, up_lin):
    return jax.nn.gelu(gate_lin, approximate=True) * up_lin


def rounded(values):
    return lax.optimization_barrier(values.astype(jnp.bfloat16)).astype(jnp.float32)


def masked_scores(query_rows, key_rows, first_pos, score_scale):
    block_rows = query_rows.shape[0]
    scores = (
        jnp.einsum("qhd,kd->hqk", query_rows, key_rows, preferred_element_type=jnp.float32)
        * score_scale
    )
    query_pos = first_pos + jnp.arange(block_rows, dtype=jnp.int32)
    key_pos = jnp.arange(key_rows.shape[0], dtype=jnp.int32)
    allowed = key_pos[None, :] <= query_pos[:, None]
    return jnp.where(allowed[None], scores, negative)


def attend_forward(queries, key_rows, value_rows, block_rows, query_offset):
    score_scale = queries.shape[-1] ** (-0.5)

    def one_block(block_index):
        row_start = block_index * block_rows
        query_rows = lax.dynamic_slice_in_dim(queries, row_start, block_rows, 0)
        scores = masked_scores(query_rows, key_rows, query_offset + row_start, score_scale)
        row_max = jnp.max(scores, -1, keepdims=True)
        exp_scores = jnp.exp(scores - row_max)
        row_total = jnp.sum(exp_scores, -1, keepdims=True)
        weights_low = (exp_scores / row_total).astype(jnp.bfloat16)
        block_out = jnp.einsum(
            "hqk,kd->qhd", weights_low, value_rows, preferred_element_type=jnp.float32
        )
        return (block_out, (row_max + jnp.log(row_total))[..., 0])

    outputs, log_totals = lax.map(
        one_block, jnp.arange(queries.shape[0] // block_rows, dtype=jnp.int32)
    )
    return (outputs.reshape(queries.shape), log_totals)


def attend_backward(queries, key_rows, value_rows, grad_rows, log_totals, block_rows, query_offset):
    score_scale = queries.shape[-1] ** (-0.5)

    def one_block(running, block_index):
        key_grad, value_grad = running
        row_start = block_index * block_rows
        query_rows = lax.dynamic_slice_in_dim(queries, row_start, block_rows, 0)
        grad_block = lax.dynamic_slice_in_dim(grad_rows, row_start, block_rows, 0)
        scores = masked_scores(query_rows, key_rows, query_offset + row_start, score_scale)
        weights = jnp.exp(scores - log_totals[block_index][..., None])
        grad_weights = jnp.einsum(
            "qhd,kd->hqk", grad_block, value_rows, preferred_element_type=jnp.float32
        )
        inner = jnp.sum(weights * grad_weights, -1, keepdims=True)
        grad_scores = (weights * (grad_weights - inner)).astype(jnp.bfloat16)
        query_grad = (
            jnp.einsum("hqk,kd->qhd", grad_scores, key_rows, preferred_element_type=jnp.float32)
            * score_scale
        )
        key_grad = (
            key_grad
            + jnp.einsum("hqk,qhd->kd", grad_scores, query_rows, preferred_element_type=jnp.float32)
            * score_scale
        )
        value_grad = value_grad + jnp.einsum(
            "hqk,qhd->kd",
            weights.astype(jnp.bfloat16),
            grad_block,
            preferred_element_type=jnp.float32,
        )
        return ((key_grad, value_grad), query_grad)

    zeros_rows = jnp.zeros(key_rows.shape, jnp.float32)
    (key_grad, value_grad), query_grads = lax.scan(
        one_block,
        (zeros_rows, zeros_rows),
        jnp.arange(queries.shape[0] // block_rows, dtype=jnp.int32),
    )
    return (query_grads.reshape(queries.shape), key_grad, value_grad)


def per_device(
    block_in,
    query_weight,
    key_weight,
    value_weight,
    output_weight,
    gate_weight,
    up_weight,
    down_weight,
    attention_norm,
    query_norm,
    key_norm,
    post_attention_norm,
    feedforward_norm,
    post_feedforward_norm,
    grad_out,
):
    gathered = (
        lax.all_gather(query_weight, "fsdp", axis=0, tiled=True),
        lax.all_gather(key_weight, "fsdp", axis=0, tiled=True),
        lax.all_gather(value_weight, "fsdp", axis=0, tiled=True),
        lax.all_gather(output_weight, "fsdp", axis=0, tiled=True),
        lax.all_gather(gate_weight, "fsdp", axis=0, tiled=True),
        lax.all_gather(up_weight, "fsdp", axis=0, tiled=True),
        lax.all_gather(down_weight, "fsdp", axis=0, tiled=True),
        lax.all_gather(attention_norm, "fsdp", axis=0, tiled=True),
        lax.all_gather(query_norm, "fsdp", axis=0, tiled=True),
        lax.all_gather(key_norm, "fsdp", axis=0, tiled=True),
        lax.all_gather(post_attention_norm, "fsdp", axis=0, tiled=True),
        lax.all_gather(feedforward_norm, "fsdp", axis=0, tiled=True),
        lax.all_gather(post_feedforward_norm, "fsdp", axis=0, tiled=True),
    )
    query_full, key_full, value_full, output_full, gate_full, up_full, down_full = gathered[:7]
    norm_gains = tuple((gain_row.astype(jnp.float32) for gain_row in gathered[7:]))
    attention_gain, query_gain, key_gain, post_attention_gain, second_gain, post_second_gain = (
        norm_gains
    )
    token_count = block_in.shape[0]
    head_size = query_gain.shape[0]
    head_count = query_full.shape[1] // head_size
    length = token_count * lax.axis_size("seq")
    block_rows = min(512, length)
    token_offset = lax.axis_index("seq") * token_count
    input_f = block_in.astype(jnp.float32)
    normed, pull_normed = jax.vjp(rms_scale, input_f, attention_gain)
    normed_low = normed.astype(jnp.bfloat16)
    query_lin = jnp.dot(normed_low, query_full, preferred_element_type=jnp.float32).reshape(
        token_count, head_count, head_size
    )
    key_lin = jnp.dot(normed_low, key_full, preferred_element_type=jnp.float32)
    value_low = jnp.dot(normed_low, value_full, preferred_element_type=jnp.float32).astype(
        jnp.bfloat16
    )
    positions = (token_offset + jnp.arange(token_count, dtype=jnp.int32)).astype(jnp.float32)
    cosine_table, sine_table = angles_for(positions, head_size)

    def query_piece(values, gain_row):
        return rotate(rms_scale(values, gain_row), cosine_table[:, None, :], sine_table[:, None, :])

    def key_piece(values, gain_row):
        return rotate(rms_scale(values, gain_row), cosine_table, sine_table)

    queries, pull_queries = jax.vjp(query_piece, query_lin, query_gain)
    key_rows, pull_keys = jax.vjp(key_piece, key_lin, key_gain)
    queries_low = queries.astype(jnp.bfloat16)
    key_all, value_all = (
        lax.all_gather(key_rows.astype(jnp.bfloat16), "seq", axis=0, tiled=True),
        lax.all_gather(value_low, "seq", axis=0, tiled=True),
    )
    query_heads = lax.all_to_all(queries_low, "seq", split_axis=1, concat_axis=0, tiled=True)
    head_out, log_totals = attend_forward(query_heads, key_all, value_all, block_rows, 0)
    mixed = lax.all_to_all(
        head_out.astype(jnp.bfloat16), "seq", split_axis=0, concat_axis=1, tiled=True
    ).reshape(token_count, head_count * head_size)
    attended = jnp.dot(mixed, output_full, preferred_element_type=jnp.float32)
    post_branch, pull_post = jax.vjp(rms_scale, attended, post_attention_gain)
    residual = input_f + post_branch
    normed_second, pull_second = jax.vjp(rms_scale, residual, second_gain)
    second_low = normed_second.astype(jnp.bfloat16)
    gate_lin = jnp.dot(second_low, gate_full, preferred_element_type=jnp.float32)
    up_lin = jnp.dot(second_low, up_full, preferred_element_type=jnp.float32)
    activated, pull_activated = jax.vjp(gelu_product, gate_lin, up_lin)
    activated_low = activated.astype(jnp.bfloat16)
    down_lin = jnp.dot(activated_low, down_full, preferred_element_type=jnp.float32)
    tail_branch, pull_tail = jax.vjp(rms_scale, down_lin, post_second_gain)
    block_out = (residual + tail_branch).astype(jnp.bfloat16)
    weights_back = (
        lax.all_gather(query_weight, "fsdp", axis=0, tiled=True),
        lax.all_gather(key_weight, "fsdp", axis=0, tiled=True),
        lax.all_gather(value_weight, "fsdp", axis=0, tiled=True),
        lax.all_gather(output_weight, "fsdp", axis=0, tiled=True),
        lax.all_gather(gate_weight, "fsdp", axis=0, tiled=True),
        lax.all_gather(up_weight, "fsdp", axis=0, tiled=True),
        lax.all_gather(down_weight, "fsdp", axis=0, tiled=True),
    )
    query_back, key_back, value_back, output_back, gate_back, up_back, down_back = weights_back
    grad_f = grad_out.astype(jnp.float32)
    grad_down, grad_post_second = pull_tail(grad_f)
    grad_down_low = grad_down.astype(jnp.bfloat16)
    grad_down_weight = jnp.einsum(
        "tf,td->fd", activated_low, grad_down_low, preferred_element_type=jnp.float32
    )
    grad_activated = jnp.einsum(
        "td,fd->tf", grad_down_low, down_back, preferred_element_type=jnp.float32
    )
    grad_gate, grad_up = pull_activated(grad_activated)
    gate_low = grad_gate.astype(jnp.bfloat16)
    up_low = grad_up.astype(jnp.bfloat16)
    grad_gate_weight = jnp.einsum(
        "td,tf->df", second_low, gate_low, preferred_element_type=jnp.float32
    )
    grad_up_weight = jnp.einsum("td,tf->df", second_low, up_low, preferred_element_type=jnp.float32)
    grad_second = jnp.einsum(
        "tf,df->td", gate_low, gate_back, preferred_element_type=jnp.float32
    ) + jnp.einsum("tf,df->td", up_low, up_back, preferred_element_type=jnp.float32)
    grad_resid_part, grad_second_gain = pull_second(grad_second)
    grad_residual = grad_f + grad_resid_part
    grad_attended, grad_post_attention = pull_post(grad_residual)
    attended_low = grad_attended.astype(jnp.bfloat16)
    grad_output_weight = jnp.einsum(
        "tq,td->qd", mixed, attended_low, preferred_element_type=jnp.float32
    )
    grad_mixed = (
        jnp.einsum("td,qd->tq", attended_low, output_back, preferred_element_type=jnp.float32)
        .astype(jnp.bfloat16)
        .reshape(token_count, head_count, head_size)
    )
    grad_head_rows = lax.all_to_all(grad_mixed, "seq", split_axis=1, concat_axis=0, tiled=True)
    query_head_grad, key_all_grad, value_all_grad = attend_backward(
        query_heads, key_all, value_all, grad_head_rows, log_totals, block_rows, 0
    )
    grad_queries = lax.all_to_all(
        query_head_grad.astype(jnp.bfloat16), "seq", split_axis=0, concat_axis=1, tiled=True
    )
    grad_keys, grad_values = (
        lax.psum_scatter(
            key_all_grad.astype(jnp.bfloat16), "seq", scatter_dimension=0, tiled=True
        ).astype(jnp.float32),
        lax.psum_scatter(
            value_all_grad.astype(jnp.bfloat16), "seq", scatter_dimension=0, tiled=True
        ).astype(jnp.float32),
    )
    grad_query_lin, grad_query_gain = pull_queries(grad_queries.astype(jnp.float32))
    grad_key_lin, grad_key_gain = pull_keys(rounded(grad_keys))
    query_lin_low = grad_query_lin.reshape(token_count, head_count * head_size).astype(jnp.bfloat16)
    key_lin_low = grad_key_lin.astype(jnp.bfloat16)
    value_lin_low = grad_values.astype(jnp.bfloat16)
    grad_query_weight = jnp.einsum(
        "td,tq->dq", normed_low, query_lin_low, preferred_element_type=jnp.float32
    )
    grad_key_weight = jnp.einsum(
        "td,tq->dq", normed_low, key_lin_low, preferred_element_type=jnp.float32
    )
    grad_value_weight = jnp.einsum(
        "td,tq->dq", normed_low, value_lin_low, preferred_element_type=jnp.float32
    )
    grad_normed = jnp.einsum(
        "tq,dq->td", query_lin_low, query_back, preferred_element_type=jnp.float32
    )
    grad_normed = grad_normed + jnp.einsum(
        "tq,dq->td", key_lin_low, key_back, preferred_element_type=jnp.float32
    )
    grad_normed = grad_normed + jnp.einsum(
        "tq,dq->td", value_lin_low, value_back, preferred_element_type=jnp.float32
    )
    grad_input_part, grad_attention_gain = pull_normed(grad_normed)
    grad_in = (grad_residual + grad_input_part).astype(jnp.bfloat16)
    scattered = (
        lax.psum_scatter(grad_query_weight, "fsdp", scatter_dimension=0, tiled=True),
        lax.psum_scatter(grad_key_weight, "fsdp", scatter_dimension=0, tiled=True),
        lax.psum_scatter(grad_value_weight, "fsdp", scatter_dimension=0, tiled=True),
        lax.psum_scatter(grad_output_weight, "fsdp", scatter_dimension=0, tiled=True),
        lax.psum_scatter(grad_gate_weight, "fsdp", scatter_dimension=0, tiled=True),
        lax.psum_scatter(grad_up_weight, "fsdp", scatter_dimension=0, tiled=True),
        lax.psum_scatter(grad_down_weight, "fsdp", scatter_dimension=0, tiled=True),
        lax.psum_scatter(grad_attention_gain, "fsdp", scatter_dimension=0, tiled=True),
        lax.psum_scatter(grad_query_gain, "fsdp", scatter_dimension=0, tiled=True),
        lax.psum_scatter(grad_key_gain, "fsdp", scatter_dimension=0, tiled=True),
        lax.psum_scatter(grad_post_attention, "fsdp", scatter_dimension=0, tiled=True),
        lax.psum_scatter(grad_second_gain, "fsdp", scatter_dimension=0, tiled=True),
        lax.psum_scatter(grad_post_second, "fsdp", scatter_dimension=0, tiled=True),
    )
    summed = (
        lax.psum(scattered[0].astype(jnp.bfloat16), "seq").astype(jnp.float32),
        lax.psum(scattered[1].astype(jnp.bfloat16), "seq").astype(jnp.float32),
        lax.psum(scattered[2].astype(jnp.bfloat16), "seq").astype(jnp.float32),
        lax.psum(scattered[3].astype(jnp.bfloat16), "seq").astype(jnp.float32),
        lax.psum(scattered[4].astype(jnp.bfloat16), "seq").astype(jnp.float32),
        lax.psum(scattered[5].astype(jnp.bfloat16), "seq").astype(jnp.float32),
        lax.psum(scattered[6].astype(jnp.bfloat16), "seq").astype(jnp.float32),
        lax.psum(scattered[7].astype(jnp.bfloat16), "seq").astype(jnp.float32),
        lax.psum(scattered[8].astype(jnp.bfloat16), "seq").astype(jnp.float32),
        lax.psum(scattered[9].astype(jnp.bfloat16), "seq").astype(jnp.float32),
        lax.psum(scattered[10].astype(jnp.bfloat16), "seq").astype(jnp.float32),
        lax.psum(scattered[11].astype(jnp.bfloat16), "seq").astype(jnp.float32),
        lax.psum(scattered[12].astype(jnp.bfloat16), "seq").astype(jnp.float32),
    )
    return (
        block_out,
        grad_in,
        summed[0],
        summed[1],
        summed[2],
        summed[3],
        summed[4],
        summed[5],
        summed[6],
        summed[7],
        summed[8],
        summed[9],
        summed[10],
        summed[11],
        summed[12],
    )


def solution(mesh):
    in_specs = (
        P(("fsdp", "seq"), None),
        P("fsdp", None),
        P("fsdp", None),
        P("fsdp", None),
        P("fsdp", None),
        P("fsdp", None),
        P("fsdp", None),
        P("fsdp", None),
        P("fsdp"),
        P("fsdp"),
        P("fsdp"),
        P("fsdp"),
        P("fsdp"),
        P("fsdp"),
        P(("fsdp", "seq"), None),
    )
    out_specs = (
        P(("fsdp", "seq"), None),
        P(("fsdp", "seq"), None),
        P("fsdp", None),
        P("fsdp", None),
        P("fsdp", None),
        P("fsdp", None),
        P("fsdp", None),
        P("fsdp", None),
        P("fsdp", None),
        P("fsdp"),
        P("fsdp"),
        P("fsdp"),
        P("fsdp"),
        P("fsdp"),
        P("fsdp"),
    )
    return jax.shard_map(
        per_device, mesh=mesh, in_specs=in_specs, out_specs=out_specs, check_vma=False
    )
```

profile of v0, /device:TPU:0, one launch (start us, length us, event | category | flops | bytes accessed | tf_op | source)
XLA Modules:
  0.0 985.4 jit_solution(9208684761553230560)
XLA Ops:
  14.0 15.8 %all-reduce.17 = (bf16[640]{0:T(1024)(128)(2,1)S(1)}, bf16[256]{0:T(256)(128)(2,1)S(1)}, bf16[256]{0:T(256)(128)(2,1)S(1)}, bf16[640]{0:T(1024)(128)(2,1)S(1)}, ...) all-reduce(bf16[640]{0:T(1024)(128)(2,1)S(1)} %dynamic-update-slice, ...), channel_id=1, replica_groups=mesh['fsdp'=8,'seq'=4] {'fsdp'}, use_global_device_ids=true, to_apply=%add.4 | all-reduce | flops 3072 | bytes 12288
  29.8 8.8 all_gather.55
  43.4 9.5 all_gather.58
  78.5 49.1 %all-gather.12.cloned.1.call-done = bf16[2560,256]{1,0:T(8,128)(2,1)} async-done(((bf16[640,256]{1,0:T(8,128)(2,1)}), bf16[2560,256]{1,0:T(8,128)(2,1)}) %all-gather.12.cloned.1.call-update) | async-done | bytes 1310736 | tf_op jit(solution)/shard_map/all_gather | solution.py:185
  128.5 35.3 %while.27 = (s32[]{:T(128)}, bf16[5,512,1,256]{3,1,2,0:T(8,128)(2,1)S(1)}, f32[5,1,512]{2,1,0:T(1,128)S(1)}, s32[5]{0:T(128)S(1)}, bf16[2560,1,256]{2,0,1:T(8,12...) while((s32[]{:T(128)}, ...), condition=%wide.region_6.7_spmd, body=%wide.region_3.6_spmd.sunk | while | flops 1353973760 | bytes 19161280 | solution.py:71
  173.9 28.6 %all-to-all-done.1 = bf16[4,2,81920]{2,1,0:T(2,128)(2,1)S(1)} async-done(((bf16[4,2,81920]{2,1,0:T(2,128)(2,1)}), bf16[4,2,81920]{2,1,0:T(2,128)(2,1)S(1)}, u32[]{:S(2)}, u32[]{:S(2)}) %all-to-all-start.1) | async-done | bytes 1310752 | tf_op jit(solution)/shard_map/all_to_all | solution.py:189
  214.0 6.6 fusion.94
  220.6 10.1 %multiply_convert_fusion.1 = (bf16[640,2048]{1,0:T(8,128)(2,1)}, f32[640,2048]{1,0:T(8,128)}) fusion(f32[640,2048]{1,0:T(8,128)} %fusion.94, bf16[640,640]{0,1:T(8,128)(2,1)} %multiply_convert_fusion.2, bf16[640,2048]{1,0:T(8,128)(2,1)} %all-gather.18.cloned.1.call-done), kind=kOutput, calls=%fused_computation.58 | convolution fusion | flops 1690828800 | bytes 16547840 | tf_op jit(solution)/shard_map/dot_general | solution.py:198
  230.7 18.3 %all-gather.20.cloned.1.call-done = bf16[2048,640]{1,0:T(8,128)(2,1)} async-done(((bf16[256,640]{1,0:T(8,128)(2,1)}), bf16[2048,640]{1,0:T(8,128)(2,1)}) %all-gather.20.cloned.1.call-update) | async-done | bytes 2621456 | tf_op jit(solution)/shard_map/all_gather | solution.py:142
  249.0 5.0 multiply_reduce_fusion.6
  258.6 6.7 multiply_convert_fusion
  281.4 31.9 %all-to-all-done.2 = bf16[640,4,256]{2,0,1:T(8,128)(2,1)} async-done(((bf16[640,4,256]{2,0,1:T(8,128)(2,1)}), bf16[640,4,256]{2,0,1:T(8,128)(2,1)}, u32[]{:S(2)}, u32[]{:S(2)}) %all-to-all-start.2) | async-done | bytes 1310752 | tf_op jit(solution)/shard_map/all_to_all | solution.py:245
  314.4 135.8 %while.28 = (s32[]{:T(128)}, f32[2560,256]{1,0:T(8,128)}, f32[2560,256]{1,0:T(8,128)}, bf16[5,512,1,256]{3,1,2,0:T(8,128)(2,1)}, s32[5]{0:T(128)S(1)}, /*index=5...) while((s32[]{:T(128)}, f32[2560,256]{1,0:T(8,128)}, ...), condition=%wide.region_15.16_spmd.clone, body=%wide.region_13.15_spmd.clone.sunk | while | flops 3371958272 | bytes 133970368 | solution.py:110
  322.5 5.0 fusion.181
  349.2 5.0 fusion.181
  376.4 5.0 fusion.181
  403.7 5.0 fusion.181
  430.9 5.0 fusion.181
  457.0 28.1 %reduce-scatter.28.cloned.1.call-done = bf16[640,256]{1,0:T(8,128)(2,1)} async-done(((bf16[2560,256]{1,0:T(8,128)(2,1)}), bf16[640,256]{1,0:T(8,128)(2,1)}) %reduce-scatter.28.cloned.1.call-update) | async-done | bytes 327696
  490.4 27.1 %reduce-scatter.12.cloned.1.call-done = bf16[640,256]{1,0:T(8,128)(2,1)} async-done(((bf16[2560,256]{1,0:T(8,128)(2,1)}), bf16[640,256]{1,0:T(8,128)(2,1)}) %reduce-scatter.12.cloned.1.call-update) | async-done | bytes 327696 | tf_op jit(solution)/shard_map/reduce_scatter | solution.py:256
  526.1 34.8 %all_to_all.60 = bf16[4,2,81920]{2,1,0:T(2,128)(2,1)} all-to-all(bf16[4,2,81920]{2,1,0:T(2,128)(2,1)S(1)} %reshape.445), channel_id=1, replica_groups=mesh['fsdp'=8,'seq'=4] {'seq'}, dimensions={0} | all-to-all | bytes 2621440 | tf_op jit(solution)/shard_map/all_to_all | solution.py:249
  573.5 6.3 fusion.98
  579.9 6.3 fusion.99
  587.4 6.6 fusion.100
  599.8 23.3 %all-reduce.16 = (bf16[640]{0:T(1024)(128)(2,1)S(1)}, bf16[256]{0:T(256)(128)(2,1)S(1)}, bf16[256]{0:T(256)(128)(2,1)S(1)}, bf16[640]{0:T(1024)(128)(2,1)S(1)}, ...) all-reduce(f32[640]{0:T(1024)S(1)} %get-tuple-element.377, ...), channel_id=11, replica_groups=mesh['fsdp'=8,'seq'=4] {'fsdp'}, use_global_device_ids=true, to_apply=%region_36.37.clone | all-reduce | flops 3072 | bytes 18432
  629.7 9.9 %reduce-scatter.20.cloned.1.call-done = f32[128,640]{1,0:T(8,128)} async-done(((f32[1024,640]{1,0:T(8,128)}), f32[128,640]{1,0:T(8,128)}) %reduce-scatter.20.cloned.1.call-update) | async-done | bytes 327696 | tf_op jit(solution)/shard_map/reduce_scatter | solution.py:289
  641.3 45.4 %reduce-scatter.14.cloned.1.call-done = f32[80,1024]{1,0:T(8,128)} async-done(((f32[640,1024]{1,0:T(8,128)}), f32[80,1024]{1,0:T(8,128)}) %reduce-scatter.14.cloned.1.call-update) | async-done | bytes 327696 | tf_op jit(solution)/shard_map/reduce_scatter | solution.py:286
  688.3 58.2 %reduce-scatter.22.cloned.1.call-done = f32[80,2048]{1,0:T(8,128)} async-done(((f32[640,2048]{1,0:T(8,128)}), f32[80,2048]{1,0:T(8,128)}) %reduce-scatter.22.cloned.1.call-update) | async-done | bytes 655376 | tf_op jit(solution)/shard_map/reduce_scatter | solution.py:290
  748.3 58.3 %reduce-scatter.24.cloned.1.call-done = f32[80,2048]{1,0:T(8,128)} async-done(((f32[640,2048]{1,0:T(8,128)}), f32[80,2048]{1,0:T(8,128)}) %reduce-scatter.24.cloned.1.call-update) | async-done | bytes 655376 | tf_op jit(solution)/shard_map/reduce_scatter | solution.py:291
  808.5 58.0 %reduce-scatter.26.cloned.1.call-done = f32[256,640]{1,0:T(8,128)} async-done(((f32[2048,640]{1,0:T(8,128)}), f32[256,640]{1,0:T(8,128)}) %reduce-scatter.26.cloned.1.call-update) | async-done | bytes 655376 | tf_op jit(solution)/shard_map/reduce_scatter | solution.py:292
  873.2 32.1 %all-reduce.23.cloned.1.call-done = (bf16[80,256]{1,0:T(8,128)(2,1)}, bf16[80,256]{1,0:T(8,128)(2,1)}, bf16[80]{0:T(256)(128)(2,1)}, bf16[32]{0:T(256)(128)(2,1)...) async-done(((bf16[80,256]{1,0:T(8,128)(2,1)}, bf16[80,256]{1,0:T(8,128)(2,1)}, bf16[80]{0:T(256)(128)(2,1)}, ...) | async-done | bytes 82704 | tf_op jit(solution)/shard_map/psum | solution.py:302
  915.0 56.3 %all-reduce.25.cloned.1.call-done = (bf16[80,1024]{1,0:T(8,128)(2,1)}, bf16[128,640]{1,0:T(8,128)(2,1)}, bf16[80,2048]{1,0:T(8,128)(2,1)}, bf16[80,2048]{1,0:T(8,128)(2,1)}, bf16[256,640]{1,0:T(8,128)(2,1)}) async-done(((bf16[80,1024]{1,0:T(8,128)(2,1)}, bf16[128,640]{1,0:T(8,128)(2,1)}, bf16[80,2048]{1,0:T(8,128)(2,1)}, bf16[80,2048]{1,0:T(8,128)(2,1)}, bf16[256,640]{1,0:T(8,128)(2,1)}), ...) | async-done | bytes 1310736 | tf_op jit(solution)/shard_map/psum | solution.py:301
  (455 shorter events, 283.8 us)
Async XLA Ops:
  7.2 22.6 %copy-start.42 = (bf16[80,256]{1,0:T(8,128)(2,1)S(1)}, bf16[80,256]{1,0:T(8,128)(2,1)}, u32[]{:S(2)}) copy-start(bf16[80,256]{1,0:T(8,128)(2,1)} %param.21) | copy-start | bytes 122884
  7.3 50.7 %all-gather.8.cloned.1.call-start = ((), (), s32[]{:S(2)}) async-start(), calls=%async_computation.13 | async-start | bytes 1474560 | tf_op jit(solution)/shard_map/all_gather | solution.py:136
  8.0 68.0 %all-gather.10.cloned.1.call-start = ((), (), s32[]{:S(2)}) async-start(), calls=%async_computation.14 | async-start | bytes 1638400 | tf_op jit(solution)/shard_map/all_gather | solution.py:184
  29.8 28.1 %copy-start.48 = (f32[640]{0:T(1024)}, f32[640]{0:T(1024)S(1)}, u32[]{:S(2)}) copy-start(f32[640]{0:T(1024)S(1)} %convert_element_type.223) | copy-start | bytes 7684
  39.5 18.4 %copy-start.50 = (f32[640]{0:T(1024)}, f32[640]{0:T(1024)S(1)}, u32[]{:S(2)}) copy-start(f32[640]{0:T(1024)S(1)} %fusion.76) | copy-start | bytes 7684
  43.3 84.3 %all-gather.12.cloned.1.call-start = ((), (), s32[]{:S(2)}) async-start(), calls=%async_computation.15 | async-start | bytes 1638400 | tf_op jit(solution)/shard_map/all_gather | solution.py:185
  54.9 153.8 %all-gather.14.cloned.1.call-start = ((), (), s32[]{:S(2)}) async-start(), calls=%async_computation.16 | async-start | bytes 1474560 | tf_op jit(solution)/shard_map/all_gather | solution.py:139
  55.5 158.5 %all-gather.16.cloned.1.call-start = ((), (), s32[]{:S(2)}) async-start(), calls=%async_computation.17 | async-start | bytes 2949120 | tf_op jit(solution)/shard_map/all_gather | solution.py:140
  70.6 57.8 %all-to-all-start = ((bf16[640,4,256]{2,0,1:T(8,128)(2,1)}), bf16[640,4,256]{2,0,1:T(8,128)(2,1)}, u32[]{:S(2)}, u32[]{:S(2)}) async-start(bf16[640,4,256]{2,0,1:T(8,128)(2,1)} %pad_maximum_fusion), calls=%async_computation | async-start | bytes 2621440 | tf_op jit(solution)/shard_map/all_to_all | solution.py:187
  75.4 145.2 %all-gather.18.cloned.1.call-start = ((), (), s32[]{:S(2)}) async-start(), calls=%async_computation.18 | async-start | bytes 2949120 | tf_op jit(solution)/shard_map/all_gather | solution.py:141
  167.7 34.8 %all-to-all-start.1 = ((bf16[4,2,81920]{2,1,0:T(2,128)(2,1)}), bf16[4,2,81920]{2,1,0:T(2,128)(2,1)S(1)}, u32[]{:S(2)}, u32[]{:S(2)}) async-start(bf16[4,2,81920]{2,1,0:T(2,128)(2,1)} %reshape.443), calls=%async_computation.1 | async-start | bytes 2621440 | tf_op jit(solution)/shard_map/all_to_all | solution.py:189
  171.2 77.8 %all-gather.20.cloned.1.call-start = ((), (), s32[]{:S(2)}) async-start(), calls=%async_computation.19 | async-start | bytes 2949120 | tf_op jit(solution)/shard_map/all_gather | solution.py:142
  276.8 36.5 %all-to-all-start.2 = ((bf16[640,4,256]{2,0,1:T(8,128)(2,1)}), bf16[640,4,256]{2,0,1:T(8,128)(2,1)}, u32[]{:S(2)}, u32[]{:S(2)}) async-start(bf16[640,4,256]{2,0,1:T(8,128)(2,1)} %bitcast.176), calls=%async_computation.2 | async-start | bytes 2621440 | tf_op jit(solution)/shard_map/all_to_all | solution.py:245
  281.4 203.7 %reduce-scatter.28.cloned.1.call-start = ((), (), s32[]{:S(2)}) async-start(), calls=%async_computation.28 | async-start | bytes 1638400
  455.6 61.9 %reduce-scatter.12.cloned.1.call-start = ((), (), s32[]{:S(2)}) async-start(), calls=%async_computation.20 | async-start | bytes 1638400 | tf_op jit(solution)/shard_map/reduce_scatter | solution.py:256
  456.9 29.4 %copy-start.45 = (f32[640]{0:T(1024)S(1)}, f32[640]{0:T(1024)}, u32[]{:S(2)}) copy-start(f32[640]{0:T(1024)} %copy-done.44) | copy-start | bytes 7684
  456.9 29.5 %copy-start.60 = (f32[128]{0:T(128)S(1)}, f32[128]{0:T(128)}, u32[]{:S(2)}) copy-start(f32[128]{0:T(128)} %copy-done.59) | copy-start | bytes 1540
  456.9 30.9 %copy-start.12 = (f32[640,256]{0,1:T(8,128)S(1)}, f32[640,256]{0,1:T(8,128)}, u32[]{:S(2)}) copy-start(f32[640,256]{0,1:T(8,128)} %copy-done.11) | copy-start | bytes 1966084
  456.9 30.9 %copy-start.41 = (f32[640]{0:T(1024)S(1)}, f32[640]{0:T(1024)}, u32[]{:S(2)}) copy-start(f32[640]{0:T(1024)} %copy-done.40) | copy-start | bytes 7684
  456.9 30.9 %copy-start.56 = (f32[256]{0:T(256)S(1)}, f32[256]{0:T(256)}, u32[]{:S(2)}) copy-start(f32[256]{0:T(256)} %copy-done.55) | copy-start | bytes 3076
  456.9 169.7 %reduce-scatter.16.cloned.1.call-start = ((), (), s32[]{:S(2)}) async-start(), calls=%async_computation.22 | async-start | bytes 737280 | tf_op jit(solution)/shard_map/reduce_scatter | solution.py:287
  490.3 29.5 %copy-start.28 = (bf16[640,4,1,256]{0,3,1,2:T(8,128)(2,1)S(1)}, bf16[640,4,1,256]{0,3,1,2:T(8,128)(2,1)}, u32[]{:S(2)}) copy-start(bf16[640,4,1,256]{0,3,1,2:T(8,128)(2,1)} %copy.171) | copy-start | bytes 3932164
  490.3 29.6 %copy-start.32 = (bf16[640,640]{0,1:T(8,128)(2,1)S(1)}, bf16[640,640]{0,1:T(8,128)(2,1)}, u32[]{:S(2)}) copy-start(bf16[640,640]{0,1:T(8,128)(2,1)} %copy-done.31) | copy-start | bytes 2457604
  490.3 137.8 %reduce-scatter.18.cloned.1.call-start = ((), (), s32[]{:S(2)}) async-start(), calls=%async_computation.23 | async-start | bytes 737280 | tf_op jit(solution)/shard_map/reduce_scatter | solution.py:288
  519.8 119.8 %reduce-scatter.20.cloned.1.call-start = ((), (), s32[]{:S(2)}) async-start(), calls=%async_computation.24 | async-start | bytes 2949120 | tf_op jit(solution)/shard_map/reduce_scatter | solution.py:289
  522.7 163.9 %reduce-scatter.14.cloned.1.call-start = ((), (), s32[]{:S(2)}) async-start(), calls=%async_computation.21 | async-start | bytes 2949120 | tf_op jit(solution)/shard_map/reduce_scatter | solution.py:286
  572.4 174.1 %reduce-scatter.22.cloned.1.call-start = ((), (), s32[]{:S(2)}) async-start(), calls=%async_computation.25 | async-start | bytes 5898240 | tf_op jit(solution)/shard_map/reduce_scatter | solution.py:290
  579.8 226.9 %reduce-scatter.24.cloned.1.call-start = ((), (), s32[]{:S(2)}) async-start(), calls=%async_computation.26 | async-start | bytes 5898240 | tf_op jit(solution)/shard_map/reduce_scatter | solution.py:291
  586.2 280.3 %reduce-scatter.26.cloned.1.call-start = ((), (), s32[]{:S(2)}) async-start(), calls=%async_computation.27 | async-start | bytes 5898240 | tf_op jit(solution)/shard_map/reduce_scatter | solution.py:292
  594.0 311.3 %all-reduce.23.cloned.1.call-start = ((), (), s32[]{:S(2)}) async-start(), calls=%async_computation.29 | async-start | bytes 169984 | tf_op jit(solution)/shard_map/psum | solution.py:302
  629.7 341.7 %all-reduce.25.cloned.1.call-start = ((), (), s32[]{:S(2)}) async-start(), calls=%async_computation.30 | async-start | bytes 2621440 | tf_op jit(solution)/shard_map/psum | solution.py:301
  748.3 120.1 %copy-start.15 = (bf16[640,640]{0,1:T(8,128)(2,1)S(1)}, bf16[640,640]{0,1:T(8,128)(2,1)}, u32[]{:S(2)}) copy-start(bf16[640,640]{0,1:T(8,128)(2,1)} %get-tuple-element.454) | copy-start | bytes 2457604
  (89 other events, 295.1 us)
Sparse Core Ops, SparseCore 0:
  10.0 28.3 all-gather.7
  43.4 32.5 all-gather.9
  78.2 49.3 all-gather.11
  129.3 23.8 all-gather.13
  154.9 30.1 all-gather.15
  186.8 30.1 all-gather.17
  218.9 30.1 all-gather.19
  455.7 29.3 reduce-scatter.27
  487.4 30.0 reduce-scatter.11
  521.0 33.3 reduce-scatter.15
  558.1 34.5 reduce-scatter.17
  595.9 43.6 reduce-scatter.19
  643.0 43.6 reduce-scatter.13
  689.9 56.5 reduce-scatter.21
  750.1 56.5 reduce-scatter.23
  809.9 56.5 reduce-scatter.25
  870.7 34.6 all-reduce.22
  909.1 62.2 all-reduce.24
where the time goes:
time: 996 us; the launch traced here: 985 us
  waiting for transfers between devices  505 us (51%)
  matrix products  203 us (20%)
  blocking collectives  92.3 us (9%)
  local copies, waits for them, and re-layouts  76 us (8%)
  other arithmetic  59.7 us (6%)
  between operations  18.2 us (2%)
  loops' own time  17.1 us (2%)
  starting transfers between devices  13.8 us (1%)
    reduce_scatter x1, waiting for transfers between devices, per_device(): lax.psum_scatter(grad_up_weight, 'fsdp', scatter_dimension=0, tiled=True)  58.3 us
    reduce_scatter x1, waiting for transfers between devices, per_device(): lax.psum_scatter(grad_gate_weight, 'fsdp', scatter_dimension=0, tiled=True)  58.2 us
    reduce_scatter x1, waiting for transfers between devices, per_device(): lax.psum_scatter(grad_down_weight, 'fsdp', scatter_dimension=0, tiled=True)  58 us
    psum x1, waiting for transfers between devices, per_device(): lax.psum(scattered[0].astype(jnp.bfloat16), 'seq').astype(jnp.float32)  56.3 us
    all_gather x1, waiting for transfers between devices, per_device(): lax.all_gather(value_low, 'seq', axis=0, tiled=True)  49.1 us
    reduce_scatter x1, waiting for transfers between devices, per_device(): lax.psum_scatter(grad_query_weight, 'fsdp', scatter_dimension=0, tiled=True)  45.4 us
    unnamed x170, local copies, waits for them, and re-layouts  42.3 us
    unnamed x2, blocking collectives  39.2 us
  transfers between devices with their start and end apart: 21, of which 15 were waited for; matrix products, arithmetic and copies ran while one was open for 17% of the time, Pallas kernels for 0%

commit v1 on v0

--- a/solution.py
+++ b/solution.py
@@ -242,7 +242,10 @@
         .astype(jnp.bfloat16)
         .reshape(token_count, head_count, head_size)
     )
-    grad_head_rows = lax.all_to_all(grad_mixed, "seq", split_axis=1, concat_axis=0, tiled=True)
+    grad_head_rows = jnp.concatenate(
+        lax.all_to_all(jnp.stack(jnp.split(grad_mixed, lax.axis_size("seq"), axis=1)), "seq", 0, 0),
+        axis=0,
+    )
     query_head_grad, key_all_grad, value_all_grad = attend_backward(
         query_heads, key_all, value_all, grad_head_rows, log_totals, block_rows, 0
     )

time: 996 us -> 999 us (level)
  transfers between devices with their start and end apart: 21 -> 21, of which waited for: 15 -> 14; matrix products, arithmetic and copies ran while one was open for 17% -> 17% of each run, Pallas kernels for 0% -> 0%
where the time goes in v1:
time: 999 us; the launch traced here: 989 us
  waiting for transfers between devices  505 us (51%)
  matrix products  203 us (20%)
  blocking collectives  92.4 us (9%)
  local copies, waits for them, and re-layouts  78.2 us (8%)
  other arithmetic  61 us (6%)
  between operations  18.4 us (2%)
  loops' own time  17.1 us (2%)
  starting transfers between devices  14 us (1%)
    reduce_scatter x1, waiting for transfers between devices, per_device(): lax.psum_scatter(grad_up_weight, 'fsdp', scatter_dimension=0, tiled=True)  58.4 us
    reduce_scatter x1, waiting for transfers between devices, per_device(): lax.psum_scatter(grad_gate_weight, 'fsdp', scatter_dimension=0, tiled=True)  58.2 us
    reduce_scatter x1, waiting for transfers between devices, per_device(): lax.psum_scatter(grad_down_weight, 'fsdp', scatter_dimension=0, tiled=True)  58 us
    psum x1, waiting for transfers between devices, per_device(): lax.psum(scattered[0].astype(jnp.bfloat16), 'seq').astype(jnp.float32)  56.2 us
    all_gather x1, waiting for transfers between devices, per_device(): lax.all_gather(value_low, 'seq', axis=0, tiled=True)  49.1 us
    reduce_scatter x1, waiting for transfers between devices, per_device(): lax.psum_scatter(grad_query_weight, 'fsdp', scatter_dimension=0, tiled=True)  45.3 us
    unnamed x170, local copies, waits for them, and re-layouts  42.4 us
    unnamed x2, blocking collectives  39.2 us
  transfers between devices with their start and end apart: 21, of which 14 were waited for; matrix products, arithmetic and copies ran while one was open for 17% of the time, Pallas kernels for 0%

profile of v1, /device:TPU:0, one launch (start us, length us, event | category | flops | bytes accessed | tf_op | source)
XLA Modules:
  0.0 988.8 jit_solution(7116260009605679735)
XLA Ops:
  14.0 15.8 %all-reduce.17 = (bf16[640]{0:T(1024)(128)(2,1)S(1)}, bf16[256]{0:T(256)(128)(2,1)S(1)}, bf16[256]{0:T(256)(128)(2,1)S(1)}, bf16[640]{0:T(1024)(128)(2,1)S(1)}, ...) all-reduce(bf16[640]{0:T(1024)(128)(2,1)S(1)} %dynamic-update-slice, ...), channel_id=1, replica_groups=mesh['fsdp'=8,'seq'=4] {'fsdp'}, use_global_device_ids=true, to_apply=%add.4 | all-reduce | flops 3072 | bytes 12288
  29.8 8.8 all_gather.55
  43.4 9.5 all_gather.58
  78.5 49.1 %all-gather.12.cloned.1.call-done = bf16[2560,256]{1,0:T(8,128)(2,1)} async-done(((bf16[640,256]{1,0:T(8,128)(2,1)}), bf16[2560,256]{1,0:T(8,128)(2,1)}) %all-gather.12.cloned.1.call-update) | async-done | bytes 1310736 | tf_op jit(solution)/shard_map/all_gather | solution.py:185
  128.5 35.3 %while.27 = (s32[]{:T(128)}, bf16[5,512,1,256]{3,1,2,0:T(8,128)(2,1)S(1)}, f32[5,1,512]{2,1,0:T(1,128)S(1)}, s32[5]{0:T(128)S(1)}, bf16[2560,1,256]{2,0,1:T(8,12...) while((s32[]{:T(128)}, ...), condition=%wide.region_6.7_spmd, body=%wide.region_3.6_spmd.sunk | while | flops 1353973760 | bytes 19161280 | solution.py:71
  173.9 28.6 %all-to-all-done.1 = bf16[4,2,81920]{2,1,0:T(2,128)(2,1)S(1)} async-done(((bf16[4,2,81920]{2,1,0:T(2,128)(2,1)}), bf16[4,2,81920]{2,1,0:T(2,128)(2,1)S(1)}, u32[]{:S(2)}, u32[]{:S(2)}) %all-to-all-start.1) | async-done | bytes 1310752 | tf_op jit(solution)/shard_map/all_to_all | solution.py:189
  214.0 6.6 fusion.95
  220.7 10.1 %multiply_convert_fusion.1 = (bf16[640,2048]{1,0:T(8,128)(2,1)}, f32[640,2048]{1,0:T(8,128)}) fusion(f32[640,2048]{1,0:T(8,128)} %fusion.95, bf16[640,640]{0,1:T(8,128)(2,1)} %multiply_convert_fusion.2, bf16[640,2048]{1,0:T(8,128)(2,1)} %all-gather.18.cloned.1.call-done), kind=kOutput, calls=%fused_computation.58 | convolution fusion | flops 1690828800 | bytes 16547840 | tf_op jit(solution)/shard_map/dot_general | solution.py:198
  230.7 18.3 %all-gather.20.cloned.1.call-done = bf16[2048,640]{1,0:T(8,128)(2,1)} async-done(((bf16[256,640]{1,0:T(8,128)(2,1)}), bf16[2048,640]{1,0:T(8,128)(2,1)}) %all-gather.20.cloned.1.call-update) | async-done | bytes 2621456 | tf_op jit(solution)/shard_map/all_gather | solution.py:142
  249.1 5.0 multiply_reduce_fusion.6
  258.6 6.4 multiply_convert_fusion
  284.6 31.9 %all-to-all-done.2 = bf16[4,640,1,256]{3,1,2,0:T(8,128)(2,1)} async-done(((bf16[4,640,1,256]{3,1,2,0:T(8,128)(2,1)}), bf16[4,640,1,256]{3,1,2,0:T(8,128)(2,1)}, u32[]{:S(2)}, u32[]{:S(2)}) %all-to-all-start.2) | async-done | bytes 1310752 | tf_op jit(solution)/shard_map/all_to_all | solution.py:246
  317.7 135.8 %while.28 = (s32[]{:T(128)}, f32[2560,256]{1,0:T(8,128)}, f32[2560,256]{1,0:T(8,128)}, bf16[5,512,1,256]{3,1,2,0:T(8,128)(2,1)}, s32[5]{0:T(128)S(1)}, /*index=5...) while((s32[]{:T(128)}, f32[2560,256]{1,0:T(8,128)}, ...), condition=%wide.region_15.16_spmd.clone, body=%wide.region_13.15_spmd.clone.sunk | while | flops 3371958272 | bytes 133970368 | solution.py:110
  325.8 5.0 fusion.182
  352.4 5.0 fusion.182
  379.7 5.0 fusion.182
  406.9 5.0 fusion.182
  434.1 5.0 fusion.182
  460.2 28.1 %reduce-scatter.28.cloned.1.call-done = bf16[640,256]{1,0:T(8,128)(2,1)} async-done(((bf16[2560,256]{1,0:T(8,128)(2,1)}), bf16[640,256]{1,0:T(8,128)(2,1)}) %reduce-scatter.28.cloned.1.call-update) | async-done | bytes 327696
  493.6 27.1 %reduce-scatter.12.cloned.1.call-done = bf16[640,256]{1,0:T(8,128)(2,1)} async-done(((bf16[2560,256]{1,0:T(8,128)(2,1)}), bf16[640,256]{1,0:T(8,128)(2,1)}) %reduce-scatter.12.cloned.1.call-update) | async-done | bytes 327696 | tf_op jit(solution)/shard_map/reduce_scatter | solution.py:259
  529.3 34.9 %all_to_all.47 = bf16[4,2,81920]{2,1,0:T(2,128)(2,1)} all-to-all(bf16[4,2,81920]{2,1,0:T(2,128)(2,1)S(1)} %reshape.449), channel_id=1, replica_groups=mesh['fsdp'=8,'seq'=4] {'seq'}, dimensions={0} | all-to-all | bytes 2621440 | tf_op jit(solution)/shard_map/all_to_all | solution.py:252
  576.8 6.3 fusion.99
  583.1 6.3 fusion.100
  590.6 6.6 fusion.101
  603.0 23.4 %all-reduce.16 = (bf16[640]{0:T(1024)(128)(2,1)S(1)}, bf16[256]{0:T(256)(128)(2,1)S(1)}, bf16[256]{0:T(256)(128)(2,1)S(1)}, bf16[640]{0:T(1024)(128)(2,1)S(1)}, ...) all-reduce(f32[640]{0:T(1024)S(1)} %get-tuple-element.377, ...), channel_id=11, replica_groups=mesh['fsdp'=8,'seq'=4] {'fsdp'}, use_global_device_ids=true, to_apply=%region_36.37.clone | all-reduce | flops 3072 | bytes 18432
  633.0 9.7 reduce-scatter.20.cloned.1.call-done
  644.5 45.3 %reduce-scatter.14.cloned.1.call-done = f32[80,1024]{1,0:T(8,128)} async-done(((f32[640,1024]{1,0:T(8,128)}), f32[80,1024]{1,0:T(8,128)}) %reduce-scatter.14.cloned.1.call-update) | async-done | bytes 327696 | tf_op jit(solution)/shard_map/reduce_scatter | solution.py:289
  691.4 58.2 %reduce-scatter.22.cloned.1.call-done = f32[80,2048]{1,0:T(8,128)} async-done(((f32[640,2048]{1,0:T(8,128)}), f32[80,2048]{1,0:T(8,128)}) %reduce-scatter.22.cloned.1.call-update) | async-done | bytes 655376 | tf_op jit(solution)/shard_map/reduce_scatter | solution.py:293
  751.4 58.4 %reduce-scatter.24.cloned.1.call-done = f32[80,2048]{1,0:T(8,128)} async-done(((f32[640,2048]{1,0:T(8,128)}), f32[80,2048]{1,0:T(8,128)}) %reduce-scatter.24.cloned.1.call-update) | async-done | bytes 655376 | tf_op jit(solution)/shard_map/reduce_scatter | solution.py:294
  811.6 58.0 %reduce-scatter.26.cloned.1.call-done = f32[256,640]{1,0:T(8,128)} async-done(((f32[2048,640]{1,0:T(8,128)}), f32[256,640]{1,0:T(8,128)}) %reduce-scatter.26.cloned.1.call-update) | async-done | bytes 655376 | tf_op jit(solution)/shard_map/reduce_scatter | solution.py:295
  876.3 32.1 %all-reduce.23.cloned.1.call-done = (bf16[80,256]{1,0:T(8,128)(2,1)}, bf16[80,256]{1,0:T(8,128)(2,1)}, bf16[80]{0:T(256)(128)(2,1)}, bf16[32]{0:T(256)(128)(2,1)...) async-done(((bf16[80,256]{1,0:T(8,128)(2,1)}, bf16[80,256]{1,0:T(8,128)(2,1)}, bf16[80]{0:T(256)(128)(2,1)}, ...) | async-done | bytes 82704 | tf_op jit(solution)/shard_map/psum | solution.py:305
  918.3 56.2 %all-reduce.25.cloned.1.call-done = (bf16[80,1024]{1,0:T(8,128)(2,1)}, bf16[128,640]{1,0:T(8,128)(2,1)}, bf16[80,2048]{1,0:T(8,128)(2,1)}, bf16[80,2048]{1,0:T(8,128)(2,1)}, bf16[256,640]{1,0:T(8,128)(2,1)}) async-done(((bf16[80,1024]{1,0:T(8,128)(2,1)}, bf16[128,640]{1,0:T(8,128)(2,1)}, bf16[80,2048]{1,0:T(8,128)(2,1)}, bf16[80,2048]{1,0:T(8,128)(2,1)}, bf16[256,640]{1,0:T(8,128)(2,1)}), ...) | async-done | bytes 1310736 | tf_op jit(solution)/shard_map/psum | solution.py:304
  (459 shorter events, 287.4 us)
Async XLA Ops:
  7.2 22.6 %copy-start.42 = (bf16[80,256]{1,0:T(8,128)(2,1)S(1)}, bf16[80,256]{1,0:T(8,128)(2,1)}, u32[]{:S(2)}) copy-start(bf16[80,256]{1,0:T(8,128)(2,1)} %param.21) | copy-start | bytes 122884
  7.3 50.7 %all-gather.8.cloned.1.call-start = ((), (), s32[]{:S(2)}) async-start(), calls=%async_computation.13 | async-start | bytes 1474560 | tf_op jit(solution)/shard_map/all_gather | solution.py:136
  8.0 68.0 %all-gather.10.cloned.1.call-start = ((), (), s32[]{:S(2)}) async-start(), calls=%async_computation.14 | async-start | bytes 1638400 | tf_op jit(solution)/shard_map/all_gather | solution.py:184
  29.8 28.1 %copy-start.48 = (f32[640]{0:T(1024)}, f32[640]{0:T(1024)S(1)}, u32[]{:S(2)}) copy-start(f32[640]{0:T(1024)S(1)} %convert_element_type.223) | copy-start | bytes 7684
  39.5 18.4 %copy-start.50 = (f32[640]{0:T(1024)}, f32[640]{0:T(1024)S(1)}, u32[]{:S(2)}) copy-start(f32[640]{0:T(1024)S(1)} %fusion.76) | copy-start | bytes 7684
  43.3 84.3 %all-gather.12.cloned.1.call-start = ((), (), s32[]{:S(2)}) async-start(), calls=%async_computation.15 | async-start | bytes 1638400 | tf_op jit(solution)/shard_map/all_gather | solution.py:185
  55.0 153.8 %all-gather.14.cloned.1.call-start = ((), (), s32[]{:S(2)}) async-start(), calls=%async_computation.16 | async-start | bytes 1474560 | tf_op jit(solution)/shard_map/all_gather | solution.py:139
  55.5 158.5 %all-gather.16.cloned.1.call-start = ((), (), s32[]{:S(2)}) async-start(), calls=%async_computation.17 | async-start | bytes 2949120 | tf_op jit(solution)/shard_map/all_gather | solution.py:140
  70.6 57.8 %all-to-all-start = ((bf16[640,4,256]{2,0,1:T(8,128)(2,1)}), bf16[640,4,256]{2,0,1:T(8,128)(2,1)}, u32[]{:S(2)}, u32[]{:S(2)}) async-start(bf16[640,4,256]{2,0,1:T(8,128)(2,1)} %pad_maximum_fusion), calls=%async_computation | async-start | bytes 2621440 | tf_op jit(solution)/shard_map/all_to_all | solution.py:187
  75.4 145.2 %all-gather.18.cloned.1.call-start = ((), (), s32[]{:S(2)}) async-start(), calls=%async_computation.18 | async-start | bytes 2949120 | tf_op jit(solution)/shard_map/all_gather | solution.py:141
  167.7 34.8 %all-to-all-start.1 = ((bf16[4,2,81920]{2,1,0:T(2,128)(2,1)}), bf16[4,2,81920]{2,1,0:T(2,128)(2,1)S(1)}, u32[]{:S(2)}, u32[]{:S(2)}) async-start(bf16[4,2,81920]{2,1,0:T(2,128)(2,1)} %reshape.447), calls=%async_computation.1 | async-start | bytes 2621440 | tf_op jit(solution)/shard_map/all_to_all | solution.py:189
  171.3 77.8 %all-gather.20.cloned.1.call-start = ((), (), s32[]{:S(2)}) async-start(), calls=%async_computation.19 | async-start | bytes 2949120 | tf_op jit(solution)/shard_map/all_gather | solution.py:142
  280.0 36.5 %all-to-all-start.2 = ((bf16[4,640,1,256]{3,1,2,0:T(8,128)(2,1)}), bf16[4,640,1,256]{3,1,2,0:T(8,128)(2,1)}, u32[]{:S(2)}, u32[]{:S(2)}) async-start(bf16[4,640,1,256]{3,1,2,0:T(8,128)(2,1)} %pad_maximum_fusion.1), calls=%async_computation.2 | async-start | bytes 2621440 | tf_op jit(solution)/shard_map/all_to_all | solution.py:246
  284.6 203.8 %reduce-scatter.28.cloned.1.call-start = ((), (), s32[]{:S(2)}) async-start(), calls=%async_computation.28 | async-start | bytes 1638400
  458.8 61.9 %reduce-scatter.12.cloned.1.call-start = ((), (), s32[]{:S(2)}) async-start(), calls=%async_computation.20 | async-start | bytes 1638400 | tf_op jit(solution)/shard_map/reduce_scatter | solution.py:259
  460.1 29.4 %copy-start.45 = (f32[640]{0:T(1024)S(1)}, f32[640]{0:T(1024)}, u32[]{:S(2)}) copy-start(f32[640]{0:T(1024)} %copy-done.44) | copy-start | bytes 7684
  460.1 29.5 %copy-start.60 = (f32[128]{0:T(128)S(1)}, f32[128]{0:T(128)}, u32[]{:S(2)}) copy-start(f32[128]{0:T(128)} %copy-done.59) | copy-start | bytes 1540
  460.2 30.9 %copy-start.12 = (f32[640,256]{0,1:T(8,128)S(1)}, f32[640,256]{0,1:T(8,128)}, u32[]{:S(2)}) copy-start(f32[640,256]{0,1:T(8,128)} %copy-done.11) | copy-start | bytes 1966084
  460.2 30.9 %copy-start.41 = (f32[640]{0:T(1024)S(1)}, f32[640]{0:T(1024)}, u32[]{:S(2)}) copy-start(f32[640]{0:T(1024)} %copy-done.40) | copy-start | bytes 7684
  460.2 30.9 %copy-start.56 = (f32[256]{0:T(256)S(1)}, f32[256]{0:T(256)}, u32[]{:S(2)}) copy-start(f32[256]{0:T(256)} %copy-done.55) | copy-start | bytes 3076
  460.2 169.8 %reduce-scatter.16.cloned.1.call-start = ((), (), s32[]{:S(2)}) async-start(), calls=%async_computation.22 | async-start | bytes 737280 | tf_op jit(solution)/shard_map/reduce_scatter | solution.py:290
  493.5 29.6 %copy-start.28 = (bf16[640,4,1,256]{0,3,1,2:T(8,128)(2,1)S(1)}, bf16[640,4,1,256]{0,3,1,2:T(8,128)(2,1)}, u32[]{:S(2)}) copy-start(bf16[640,4,1,256]{0,3,1,2:T(8,128)(2,1)} %copy.188) | copy-start | bytes 3932164
  493.5 29.6 %copy-start.32 = (bf16[640,640]{0,1:T(8,128)(2,1)S(1)}, bf16[640,640]{0,1:T(8,128)(2,1)}, u32[]{:S(2)}) copy-start(bf16[640,640]{0,1:T(8,128)(2,1)} %copy-done.31) | copy-start | bytes 2457604
  493.6 137.9 %reduce-scatter.18.cloned.1.call-start = ((), (), s32[]{:S(2)}) async-start(), calls=%async_computation.23 | async-start | bytes 737280 | tf_op jit(solution)/shard_map/reduce_scatter | solution.py:291
  523.0 119.8 %reduce-scatter.20.cloned.1.call-start = ((), (), s32[]{:S(2)}) async-start(), calls=%async_computation.24 | async-start | bytes 2949120 | tf_op jit(solution)/shard_map/reduce_scatter | solution.py:292
  526.0 163.8 %reduce-scatter.14.cloned.1.call-start = ((), (), s32[]{:S(2)}) async-start(), calls=%async_computation.21 | async-start | bytes 2949120 | tf_op jit(solution)/shard_map/reduce_scatter | solution.py:289
  575.7 173.9 %reduce-scatter.22.cloned.1.call-start = ((), (), s32[]{:S(2)}) async-start(), calls=%async_computation.25 | async-start | bytes 5898240 | tf_op jit(solution)/shard_map/reduce_scatter | solution.py:293
  583.1 226.7 %reduce-scatter.24.cloned.1.call-start = ((), (), s32[]{:S(2)}) async-start(), calls=%async_computation.26 | async-start | bytes 5898240 | tf_op jit(solution)/shard_map/reduce_scatter | solution.py:294
  589.5 280.1 %reduce-scatter.26.cloned.1.call-start = ((), (), s32[]{:S(2)}) async-start(), calls=%async_computation.27 | async-start | bytes 5898240 | tf_op jit(solution)/shard_map/reduce_scatter | solution.py:295
  597.3 311.2 %all-reduce.23.cloned.1.call-start = ((), (), s32[]{:S(2)}) async-start(), calls=%async_computation.29 | async-start | bytes 169984 | tf_op jit(solution)/shard_map/psum | solution.py:305
  633.0 341.4 %all-reduce.25.cloned.1.call-start = ((), (), s32[]{:S(2)}) async-start(), calls=%async_computation.30 | async-start | bytes 2621440 | tf_op jit(solution)/shard_map/psum | solution.py:304
  751.4 120.1 %copy-start.15 = (bf16[640,640]{0,1:T(8,128)(2,1)S(1)}, bf16[640,640]{0,1:T(8,128)(2,1)}, u32[]{:S(2)}) copy-start(bf16[640,640]{0,1:T(8,128)(2,1)} %get-tuple-element.454) | copy-start | bytes 2457604
  (89 other events, 294.4 us)
Sparse Core Ops, SparseCore 0:
  10.0 28.3 all-gather.7
  43.4 32.5 all-gather.9
  78.2 49.3 all-gather.11
  129.3 23.8 all-gather.13
  155.0 30.1 all-gather.15
  186.9 30.1 all-gather.17
  218.9 30.1 all-gather.19
  459.0 29.3 reduce-scatter.27
  490.6 30.0 reduce-scatter.11
  524.3 33.3 reduce-scatter.15
  561.3 34.5 reduce-scatter.17
  599.1 43.6 reduce-scatter.19
  646.1 43.5 reduce-scatter.13
  693.0 56.5 reduce-scatter.21
  753.2 56.5 reduce-scatter.23
  813.0 56.5 reduce-scatter.25
  873.8 34.6 all-reduce.22
  912.2 62.2 all-reduce.24
